TPU v7x, 32 devices: a whole 2x2x4 slice. The times are simulated.
32 devices in a mesh: fsdp: 8 (over z, y), seq: 4 (over x, core).
Axes of the slice: x: 2, y: 2, z: 4, core: 2. Of those that a mesh axis runs over, the one named last changes fastest.
Arguments:
- tokens: bfloat16 [8, 512, 8192], P('fsdp', 'seq'), may hold values from -6 to 6
- queries: bfloat16 [8, 512, 8192], P('fsdp', None, 'seq'), may hold values from -6 to 6
- key_weight: bfloat16 [8192, 1024], P('fsdp', 'seq'), may hold values from -1 to 1
- u_factor: float32 [8192, 64], P('fsdp'), may hold values from -6 to 6
- v_factor: float32 [1024, 64], replicated, may hold values from -6 to 6
Outputs:
- update: float32 [8192, 1024], P('fsdp')
- losses: float32 [2], replicated
All inputs are finite; a program needn't handle non-finite values.
Results may differ from a plain program's by a relative error of at most 0.0003.
Values may be sent and summed in bfloat16 or wider, within the bound.
A program may use at most 64 MiB of HBM per device.

v0:
```python
import math

import jax
import jax.numpy as jnp
from jax import lax
from jax.sharding import PartitionSpec as P

D = 8192
HQ = 64
HD = 128
R = 64
KD = 1024
GROUP = 8


def highest(left, right):
    return jnp.dot(left, right, precision=lax.Precision.HIGHEST, preferred_element_type=jnp.float32)


def solve_rows(rows, gram):
    lower = jnp.linalg.cholesky(gram)
    return lax.linalg.triangular_solve(lower, rows, left_side=False, lower=True, transpose_a=True)


def local(tokens, queries, key_weight, u_factor, v_factor):
    q_v = v_factor
    for turn in range(2):
        q_v = solve_rows(q_v, highest(q_v.T, q_v))
    u_rows = u_factor
    for turn in range(2):
        whole_u = lax.all_gather(u_rows, "fsdp", axis=0, tiled=True)
        u_rows = solve_rows(u_rows, highest(whole_u.T, whole_u))
    q_low = u_rows.astype(jnp.bfloat16)
    whole_x = lax.all_gather(tokens, "seq", axis=1, tiled=True)[0]
    length = whole_x.shape[0]
    slice_width = key_weight.shape[1]
    weight_piece = lax.all_gather(key_weight, "fsdp", axis=0, tiled=True)
    factor_piece = lax.all_gather(q_low, "fsdp", axis=0, tiled=True)
    base = jnp.dot(whole_x, weight_piece, preferred_element_type=jnp.float32)
    side = jnp.dot(whole_x, factor_piece, preferred_element_type=jnp.float32)
    col_start = lax.axis_index("seq") * slice_width
    v_slice = lax.dynamic_slice_in_dim(q_v, col_start, slice_width, 0)
    offset = 2.0 * highest(side, v_slice.T)
    keys = jnp.stack([base + offset, base - offset]).astype(jnp.bfloat16)
    local_kv = slice_width // HD
    query_rows = queries[0]
    query_heads = query_rows.reshape(length, local_kv, GROUP, HD).transpose(1, 2, 0, 3)
    key_heads = keys.reshape(2, length, local_kv, HD).transpose(2, 0, 1, 3)
    places = jnp.arange(length)
    causal = places[:, None] >= places[None, :]
    factor_scale = 1.0 / math.sqrt(HD)

    def one_query_head(query_one, key_one):
        scores = (
            jnp.einsum("td,npd->ntp", query_one, key_one, preferred_element_type=jnp.float32)
            * factor_scale
        )
        scores = jnp.where(causal[None], scores, -1e30)
        top = jnp.max(scores, axis=-1)
        total = jnp.sum(jnp.where(causal[None], jnp.exp(scores - top[..., None]), 0.0), axis=-1)
        return jnp.sum(top + jnp.log(total), axis=1)

    def one_key_head(pair):
        group_queries, key_one = pair
        return jnp.sum(
            lax.map(lambda query_one: one_query_head(query_one, key_one), group_queries), axis=0
        )

    partial_sums = jnp.sum(lax.map(one_key_head, (query_heads, key_heads)), axis=0)
    sums = lax.psum(partial_sums, ("fsdp", "seq"))
    losses = sums / (lax.axis_size("fsdp") * length * HQ)
    unit = math.sqrt(D * KD / R)
    update = unit * highest(u_rows, q_v.T)
    return (update, losses)


def solution(mesh):
    in_specs = (
        P("fsdp", "seq", None),
        P("fsdp", None, "seq"),
        P("fsdp", "seq"),
        P("fsdp", None),
        P(),
    )
    out_specs = (P("fsdp", None), P())
    return jax.shard_map(local, mesh=mesh, in_specs=in_specs, out_specs=out_specs, check_vma=False)
```

profile of v0, /device:TPU:0, one launch (start us, length us, event | category | flops | bytes accessed | tf_op | source)
XLA Modules:
  0.0 401.8 jit_solution(12555613587642206902)
XLA Ops:
  7.2 0.7 all-gather.6.cloned.1.call-update
  8.0 54.2 %all-gather.6.cloned.1.call-done = f32[8192,64]{0,1:T(8,128)} async-done(((f32[1024,64]{0,1:T(8,128)}), f32[8192,64]{0,1:T(8,128)}) %all-gather.6.cloned.1.call-update) | async-done | bytes 2097168 | tf_op jit(solution)/shard_map/all_gather | solution.py:31
  62.2 4.0 %fusion.30 = f32[64,64]{1,0:T(8,128)S(1)} fusion(f32[8192,64]{0,1:T(8,128)} %all-gather.6.cloned.1.call-done), kind=kOutput, calls=%fused_computation.63 | convolution fusion | flops 402653184 | bytes 2113536 | tf_op jit(solution)/shard_map/dot_general | solution.py:17
  66.3 5.8 %cholesky.74 = f32[64,64]{1,0:T(8,128)S(1)} custom-call(f32[64,64]{1,0:T(8,128)S(1)} %fusion.25), custom_call_target="Cholesky" | custom-call | tf_op jit(solution)/shard_map/jit(cholesky)/cholesky | solution.py:21
  72.2 0.6 compare_reduce_fusion.3
  72.9 0.7 fusion.14
  73.5 4.9 %custom-call.8 = f32[1,64,64]{1,2,0:T(8,128)S(1)} custom-call(f32[1,64,64]{2,1,0:T(8,128)S(1)} %fusion.14), custom_call_target="InvertDiagBlocksLowerTriangular" | custom-call | tf_op jit(solution)/shard_map/triangular_solve/custom-call.0 | solution.py:22
  78.4 1.1 convolution_bitcast_fusion.3
  79.6 47.9 %all-gather.8.cloned.1.call-done = f32[8192,64]{0,1:T(8,128)} async-done(((f32[1024,64]{0,1:T(8,128)}), f32[8192,64]{0,1:T(8,128)}) %all-gather.8.cloned.1.call-update) | async-done | bytes 2097168 | tf_op jit(solution)/shard_map/all_gather | solution.py:31
  127.5 4.0 %fusion.31 = f32[64,64]{1,0:T(8,128)S(1)} fusion(f32[8192,64]{0,1:T(8,128)} %all-gather.8.cloned.1.call-done), kind=kOutput, calls=%fused_computation.64 | convolution fusion | flops 402653184 | bytes 2113536 | tf_op jit(solution)/shard_map/dot_general | solution.py:17
  131.6 5.8 %cholesky.85 = f32[64,64]{1,0:T(8,128)S(1)} custom-call(f32[64,64]{1,0:T(8,128)S(1)} %fusion.23), custom_call_target="Cholesky" | custom-call | tf_op jit(solution)/shard_map/jit(cholesky)/cholesky | solution.py:21
  137.5 0.6 compare_reduce_fusion.2
  138.1 0.7 fusion.15
  138.8 4.9 %custom-call.9 = f32[1,64,64]{1,2,0:T(8,128)S(1)} custom-call(f32[1,64,64]{2,1,0:T(8,128)S(1)} %fusion.15), custom_call_target="InvertDiagBlocksLowerTriangular" | custom-call | tf_op jit(solution)/shard_map/triangular_solve/custom-call.0 | solution.py:22
  143.7 1.1 fusion.29
  146.5 5.8 %cholesky.96 = f32[64,64]{1,0:T(8,128)S(1)} custom-call(f32[64,64]{1,0:T(8,128)S(1)} %fusion.21), custom_call_target="Cholesky" | custom-call | tf_op jit(solution)/shard_map/jit(cholesky)/cholesky | solution.py:21
  152.4 0.6 compare_reduce_fusion.1
  153.0 0.7 fusion.16
  153.7 4.9 %custom-call.10 = f32[1,64,64]{1,2,0:T(8,128)S(1)} custom-call(f32[1,64,64]{2,1,0:T(8,128)S(1)} %fusion.16), custom_call_target="InvertDiagBlocksLowerTriangular" | custom-call | tf_op jit(solution)/shard_map/triangular_solve/custom-call.0 | solution.py:22
  159.5 5.9 %cholesky.107 = f32[64,64]{1,0:T(8,128)S(1)} custom-call(f32[64,64]{1,0:T(8,128)S(1)} %fusion.19), custom_call_target="Cholesky" | custom-call | tf_op jit(solution)/shard_map/jit(cholesky)/cholesky | solution.py:21
  165.3 0.6 compare_reduce_fusion
  166.0 0.7 fusion.17
  166.6 4.9 %custom-call.11 = f32[1,64,64]{1,2,0:T(8,128)S(1)} custom-call(f32[1,64,64]{2,1,0:T(8,128)S(1)} %fusion.17), custom_call_target="InvertDiagBlocksLowerTriangular" | custom-call | tf_op jit(solution)/shard_map/triangular_solve/custom-call.0 | solution.py:22
  171.6 2.5 copy.17
  174.5 10.1 %all-gather.14.cloned.1.call-done = bf16[8192,64]{0,1:T(8,128)(2,1)} async-done(((bf16[1024,64]{0,1:T(8,128)(2,1)}), bf16[8192,64]{0,1:T(8,128)(2,1)}) %all-gather.14.cloned.1.call-update) | async-done | bytes 1048592 | tf_op jit(solution)/shard_map/all_gather | solution.py:38
  184.6 58.4 %all-gather.10.cloned.1.call-done = bf16[1,512,8192]{2,1,0:T(8,128)(2,1)} async-done(((bf16[1,128,8192]{2,1,0:T(8,128)(2,1)}), bf16[1,512,8192]{2,1,0:T(8,128)(2,1)}) %all-gather.10.cloned.1.call-update) | async-done | bytes 8388624 | tf_op jit(solution)/shard_map/all_gather | solution.py:34
  243.0 6.4 %fusion.9 = f32[64,512]{1,0:T(8,128)S(1)} fusion(bf16[8192,64]{0,1:T(8,128)(2,1)} %all-gather.14.cloned.1.call-done, bf16[1,512,8192]{2,1,0:T(8,128)(2,1)} %all-gather.10.cloned.1.call-done), kind=kOutput, calls=%fused_computation.15 | convolution fusion | flops 536870912 | bytes 9568256 | tf_op jit(solution)/shard_map/dot_general | solution.py:40
  249.4 0.6 convolution_multiply_fusion.1
  250.0 68.4 %all-gather.12.cloned.1.call-done = bf16[8192,256]{1,0:T(8,128)(2,1)} async-done(((bf16[1024,256]{1,0:T(8,128)(2,1)}), bf16[8192,256]{1,0:T(8,128)(2,1)}) %all-gather.12.cloned.1.call-update) | async-done | bytes 4194320 | tf_op jit(solution)/shard_map/all_gather | solution.py:37
  318.4 6.9 %add_convert_fusion = (bf16[512,256]{0,1:T(8,128)(2,1)S(1)}, bf16[512,256]{0,1:T(8,128)(2,1)S(1)}) fusion(f32[512,256]{0,1:T(8,128)S(1)} %convolution_multiply_fusion.1, bf16[8192,256]{1,0:T(8,128)(2,1)} %all-gather.12.cloned.1.call-done, bf16[1,512,8192]{2,1,0:T(8,128)(2,1)} %all-gather.10.cloned.1.call-done), kind=kOutput, calls=%fused_computation.27 | convolution fusion | flops 2148007936 | bytes 13631488 | tf_op jit(solution)/shard_map/dot_general | solution.py:39
  325.8 25.3 %while.26 = (s32[]{:T(128)}, f32[2,2]{1,0:T(2,128)S(1)}, bf16[2,8,512,128]{2,3,1,0:T(8,128)(2,1)}, bf16[2,2,512,128]{3,2,1,0:T(8,128)(2,1)S(1)}, s32[]{:T(128)},...) while((s32[]{:T(128)}, f32[2,2]{1,0:T(2,128)S(1)}, ...), condition=%wide.region_9.12_spmd.clone.clone, body=%wide.region_2.11_spmd.clone.clone.sunk | while | flops 138674192 | bytes 10113394 | solution.py:69
  325.8 1.3 constant_dynamic-slice_fusion.2
  327.1 0.7 copy.23
  327.9 10.4 %while.27 = (s32[]{:T(128)}, f32[8,2]{1,0:T(8,128)S(1)}, pred[512,512]{0,1:T(8,128)(4,1)S(1)}, bf16[8,512,128]{2,1,0:T(8,128)(2,1)S(1)}, bf16[2,512,128]{2,1,0:T(8,128)(2,1)S(1)}, /*index=5*/s32[]{:T(128)}, s32[]{:T(128)}) while((s32[]{:T(128)}, f32[8,2]{1,0:T(8,128)S(1)}, pred[512,512]{0,1:T(8,128)(4,1)S(1)}, ...), condition=%wide.region_7.9_spmd.clone, body=%wide.region_3.8_spmd.clone.sunk | while | flops 138412032 | bytes 5132397 | solution.py:66
  328.5 0.6 fusion.55
  329.8 0.6 fusion.55
  331.1 0.6 fusion.55
  335.0 0.6 fusion.55
  336.3 0.6 fusion.55
  337.6 0.6 fusion.55
  338.4 1.3 constant_dynamic-slice_fusion.2
  339.8 0.7 copy.23
  340.6 10.4 %while.27 = (s32[]{:T(128)}, f32[8,2]{1,0:T(8,128)S(1)}, pred[512,512]{0,1:T(8,128)(4,1)S(1)}, bf16[8,512,128]{2,1,0:T(8,128)(2,1)S(1)}, bf16[2,512,128]{2,1,0:T(8,128)(2,1)S(1)}, /*index=5*/s32[]{:T(128)}, s32[]{:T(128)}) while((s32[]{:T(128)}, f32[8,2]{1,0:T(8,128)S(1)}, pred[512,512]{0,1:T(8,128)(4,1)S(1)}, ...), condition=%wide.region_7.9_spmd.clone, body=%wide.region_3.8_spmd.clone.sunk | while | flops 138412032 | bytes 5132397 | solution.py:66
  341.2 0.6 fusion.55
  342.5 0.6 fusion.55
  343.8 0.6 fusion.55
  351.1 5.1 %convolution_multiply_fusion = f32[1024,1024]{1,0:T(8,128)} fusion(f32[1024,64]{0,1:T(8,128)S(1)} %get-tuple-element.132, f32[1024,64]{0,1:T(8,128)S(1)} %convolution_bitcast_fusion), kind=kOutput, calls=%fused_computation.19 | convolution fusion | flops 806354944 | bytes 4718592 | tf_op jit(solution)/shard_map/dot_general | solution.py:17
  356.2 38.5 %psum.7 = f32[2]{0:T(128)S(1)} all-reduce(f32[2]{0:T(128)S(1)} %reduce_sum.36), channel_id=1, replica_groups=mesh['fsdp'=8,'seq'=4] {'fsdp','seq'}, use_global_device_ids=true, to_apply=%region_11.14 | all-reduce | flops 2 | bytes 16 | tf_op jit(solution)/shard_map/psum | solution.py:70
  (104 shorter events, 20.0 us)
Async XLA Ops:
  7.2 138.8 %copy-start = (f32[1024,64]{0,1:T(8,128)S(1)}, f32[1024,64]{0,1:T(8,128)}, u32[]{:S(2)}) copy-start(f32[1024,64]{0,1:T(8,128)} %param.16) | copy-start | bytes 786436
  7.2 55.0 %all-gather.6.cloned.1.call-start = ((), (), s32[]{:S(2)}) async-start(), calls=%async_computation | async-start | bytes 2359296 | tf_op jit(solution)/shard_map/all_gather | solution.py:31
  7.9 70.5 %copy-start.3 = (f32[1024,64]{0,1:T(8,128)S(1)}, f32[1024,64]{0,1:T(8,128)}, u32[]{:S(2)}) copy-start(f32[1024,64]{0,1:T(8,128)} %param.15) | copy-start | bytes 786436
  7.9 119.6 %all-gather.8.cloned.1.call-start = ((), (), s32[]{:S(2)}) async-start(), calls=%async_computation.1 | async-start | bytes 2359296 | tf_op jit(solution)/shard_map/all_gather | solution.py:31
  79.6 64.1 %copy-start.1 = (f32[1024,64]{0,1:T(8,128)S(1)}, f32[1024,64]{0,1:T(8,128)}, u32[]{:S(2)}) copy-start(f32[1024,64]{0,1:T(8,128)} %convolution_bitcast_fusion.3) | copy-start | bytes 786436
  79.6 105.0 %all-gather.14.cloned.1.call-start = ((), (), s32[]{:S(2)}) async-start(), calls=%async_computation.4 | async-start | bytes 1179648 | tf_op jit(solution)/shard_map/all_gather | solution.py:38
  144.8 26.7 %copy-start.2 = (bf16[1,512,2048]{2,1,0:T(8,128)(2,1)S(1)}, bf16[1,512,2048]{2,1,0:T(8,128)(2,1)}, u32[]{:S(2)}) copy-start(bf16[1,512,2048]{2,1,0:T(8,128)(2,1)} %param.13) | copy-start | bytes 6291460
  144.8 98.2 %all-gather.10.cloned.1.call-start = ((), (), s32[]{:S(2)}) async-start(), calls=%async_computation.2 | async-start | bytes 10485760 | tf_op jit(solution)/shard_map/all_gather | solution.py:34
  145.4 173.0 %all-gather.12.cloned.1.call-start = ((), (), s32[]{:S(2)}) async-start(), calls=%async_computation.3 | async-start | bytes 4718592 | tf_op jit(solution)/shard_map/all_gather | solution.py:37
Sparse Core Ops, SparseCore 0:
  10.2 51.9 all-gather.5
  79.7 47.7 all-gather.7
  144.9 39.6 all-gather.13
  186.0 56.9 all-gather.9
  245.0 73.3 all-gather.11
where the time goes:
time: 402 us
  waiting for transfers between devices  241 us (60%)
  other arithmetic  60.3 us (15%)
  matrix products  39.7 us (10%)
  blocking collectives  38.5 us (10%)
  between operations  14 us (3%)
  local copies, waits for them, and re-layouts  7.84 us (2%)
    all_gather x2, waiting for transfers between devices, local(): whole_u = lax.all_gather(u_rows, 'fsdp', axis=0, tiled=True)  102 us
    all_gather x1, waiting for transfers between devices, local(): weight_piece = lax.all_gather(key_weight, 'fsdp', axis=0, tiled=True)  68.4 us
    all_gather x1, waiting for transfers between devices, local(): whole_x = lax.all_gather(tokens, 'seq', axis=1, tiled=True)[0]  58.4 us
    psum x1, blocking collectives, local(): sums = lax.psum(partial_sums, ('fsdp', 'seq'))  38.5 us
    another operation x12, other arithmetic, solve_rows(): lower = jnp.linalg.cholesky(gram)  26.1 us
    another operation x8, other arithmetic, solve_rows(): lax.linalg.triangular_solve(lower, rows, left_side=False, lower=True, tra...  22.2 us
    dot_general x6, matrix products, highest(): jnp.dot(left, right, precision=lax.Precision.HIGHEST, preferred_element_t...  14.5 us
    all_gather x1, waiting for transfers between devices, local(): factor_piece = lax.all_gather(q_low, 'fsdp', axis=0, tiled=True)  10.1 us
  transfers between devices with their start and end apart: 5, of which 5 were waited for; matrix products, arithmetic and copies ran while one was open for 9% of the time, Pallas kernels for 0%

commit v1 on v0

v1 whole, which is shorter than its diff:
```python
import functools
import math

import jax
import jax.numpy as jnp
from jax import lax
from jax.experimental import pallas as pl
from jax.experimental.pallas import tpu as pltpu
from jax.sharding import PartitionSpec as P

D = 8192
HQ = 64
HD = 128
R = 64
KD = 1024
GROUP = 8
CHUNKS = 4
KT = 1024
BF = jnp.bfloat16
F32 = jnp.float32
MESH = pl.DeviceIdType.MESH
VMEM = pl.BlockSpec(memory_space=pltpu.VMEM)
ANY = pl.BlockSpec(memory_space=pl.ANY)


def dot(left, right, contract, precision=None):
    return lax.dot_general(left, right, ((contract[0], contract[1]), ((), ())), precision=precision, preferred_element_type=F32)


def exact(left, right, contract):
    return dot(left, right, contract, lax.Precision.HIGHEST)


def inverse_factors(grams):
    rows = lax.broadcasted_iota(jnp.int32, (R, 2 * R), 0)
    lanes = lax.broadcasted_iota(jnp.int32, (R, 2 * R), 1)
    unit = (lanes == rows + R).astype(F32)
    work = [jnp.concatenate([g, jnp.zeros((R, R), F32)], axis=1) + unit for g in grams]
    scales = [jnp.ones((R, 1), F32) for _ in grams]
    column_rows = lax.broadcasted_iota(jnp.int32, (R, 1), 0)
    for j in range(R):
        for n in range(len(work)):
            a = work[n]
            row = a[j : j + 1, :]
            column = a[:, j : j + 1]
            pivot = a[j : j + 1, j : j + 1]
            factor = jnp.where(column_rows > j, column * (1.0 / pivot), 0.0)
            scales[n] = jnp.where(column_rows == j, pivot, scales[n])
            work[n] = a - factor * row
    return [(a * lax.rsqrt(s))[:, R:] for a, s in zip(work, scales)]


def keys_kernel(nf, ns, x_hbm, w_hbm, u_ref, v_ref, keys_ref, qu_ref, qv_ref, xs, ws, qp, ql, gm, acc, sacc,
                in_sem, g_send, g_recv, q_send, q_recv, up_send, up_recv, dn_send, dn_recv, p_send, p_recv,
                b_send, b_recv, n_send, n_recv, r_send, r_recv):
    f = lax.axis_index("fsdp")
    s = lax.axis_index("seq")
    line = nf // 2
    a, b = f // 2, lax.rem(f, 2)
    mate = 2 * a + (1 - b)
    core = lax.rem(s, 2)
    brother = s - core + (1 - core)
    across = lax.rem(s + 2, ns)
    rows = u_ref.shape[0]
    half = rows // 2
    plen = xs.shape[0] // ns
    width = D // CHUNKS
    cols = ws.shape[1]

    load_x = pltpu.make_async_copy(x_hbm.at[0], xs.at[pl.ds(pl.multiple_of(s * plen, plen), plen), :], in_sem.at[0])
    load_w = pltpu.make_async_copy(w_hbm, ws.at[pl.ds(pl.multiple_of(f * rows, rows), rows), :], in_sem.at[1])
    load_x.start()
    load_w.start()

    barrier = pltpu.get_barrier_semaphore()

    @pl.loop(1, nf)
    def _(d):
        pl.semaphore_signal(barrier, inc=1, device_id=(lax.rem(f + d, nf), s), device_id_type=MESH)

    @pl.loop(1, ns)
    def _(d):
        pl.semaphore_signal(barrier, inc=1, device_id=(f, lax.rem(s + d, ns)), device_id_type=MESH)

    gram_v = exact(v_ref[...], v_ref[...], ((0,), (0,)))
    gram_u = exact(u_ref[...], u_ref[...], ((0,), (0,)))
    pl.semaphore_wait(barrier, nf - 1 + ns - 1)

    def gram_copy(turn, d):
        return pltpu.make_async_remote_copy(
            src_ref=gm.at[turn, f], dst_ref=gm.at[turn, f], send_sem=g_send.at[turn, d], recv_sem=g_recv.at[turn, d],
            device_id=(lax.rem(f + d, nf), s), device_id_type=MESH)

    def gram_arrival(turn, d):
        source = lax.rem(f + nf - d, nf)
        return pltpu.make_async_remote_copy(
            src_ref=gm.at[turn, source], dst_ref=gm.at[turn, source], send_sem=g_send.at[turn, d],
            recv_sem=g_recv.at[turn, d], device_id=(lax.rem(f + d, nf), s), device_id_type=MESH)

    def send_gram(turn, gram):
        gm[turn, f] = gram

        @pl.loop(1, nf)
        def _(d):
            gram_copy(turn, d).start()

    def sum_gram(turn):
        @pl.loop(1, nf)
        def _(d):
            gram_arrival(turn, d).wait_recv()

        return jnp.sum(gm[turn], axis=0)

    def block(index):
        return ws.at[pl.ds(pl.multiple_of(index * rows, rows), rows), :]

    def up(k):
        piece = block(2 * (a - k + 1) + b)
        return pltpu.make_async_remote_copy(src_ref=piece, dst_ref=piece, send_sem=up_send.at[k], recv_sem=up_recv.at[k],
                                            device_id=(f + 2, s), device_id_type=MESH)

    def down(k):
        piece = block(2 * (a + k - 1) + b)
        return pltpu.make_async_remote_copy(src_ref=piece, dst_ref=piece, send_sem=dn_send.at[k], recv_sem=dn_recv.at[k],
                                            device_id=(f - 2, s), device_id_type=MESH)

    def pair(at):
        piece = block(2 * at + b)
        return pltpu.make_async_remote_copy(src_ref=piece, dst_ref=piece, send_sem=p_send.at[at], recv_sem=p_recv.at[at],
                                            device_id=(mate, s), device_id_type=MESH)

    def pair_arrival(at):
        piece = block(2 * at + (1 - b))
        return pltpu.make_async_remote_copy(src_ref=piece, dst_ref=piece, send_sem=p_send.at[at], recv_sem=p_recv.at[at],
                                            device_id=(mate, s), device_id_type=MESH)

    def sends(k):
        @pl.when((a + 1 < line) & (a - k + 1 >= 0))
        def _():
            up(k).start()

        @pl.when((a > 0) & (a + k - 1 < line))
        def _():
            down(k).start()

    def relay(k):
        @pl.when(a - k >= 0)
        def _():
            piece = block(2 * (a - k) + b)
            pltpu.make_async_remote_copy(src_ref=piece, dst_ref=piece, send_sem=up_send.at[k], recv_sem=up_recv.at[k],
                                         device_id=(mate, s), device_id_type=MESH).wait_recv()

        @pl.when(a + k < line)
        def _():
            piece = block(2 * (a + k) + b)
            pltpu.make_async_remote_copy(src_ref=piece, dst_ref=piece, send_sem=dn_send.at[k], recv_sem=dn_recv.at[k],
                                         device_id=(mate, s), device_id_type=MESH).wait_recv()

        sends(k + 1)

        @pl.when(a - k >= 0)
        def _():
            pair(a - k).start()

        @pl.when(a + k < line)
        def _():
            pair(a + k).start()

    def tokens(owner, chunk):
        return xs.at[pl.ds(pl.multiple_of(owner * plen, plen), plen), pl.ds(chunk * width, width)]

    def token_copy(owner, chunk, to, send, recv):
        piece = tokens(owner, chunk)
        return pltpu.make_async_remote_copy(src_ref=piece, dst_ref=piece, send_sem=send.at[chunk], recv_sem=recv.at[chunk],
                                            device_id=(f, to), device_id_type=MESH)

    def pass_on(chunk):
        token_copy(across, chunk, across, n_send, n_recv).wait_recv()
        token_copy(across, chunk, brother, r_send, r_recv).start()

    send_gram(0, gram_u)
    load_w.wait()
    sends(1)
    pair(a).start()
    load_x.wait()
    for chunk in range(CHUNKS):
        token_copy(s, chunk, across, n_send, n_recv).start()
    for chunk in range(CHUNKS):
        token_copy(s, chunk, brother, b_send, b_recv).start()

    inv_u, inv_v = inverse_factors([sum_gram(0), gram_v])
    qu_ref[...] = exact(u_ref[...], inv_u, ((1,), (1,)))
    send_gram(1, exact(qu_ref[...], qu_ref[...], ((0,), (0,))))
    qv_ref[...] = exact(v_ref[...], inv_v, ((1,), (1,)))
    gram_v = exact(qv_ref[...], qv_ref[...], ((0,), (0,)))
    relay(1)
    pass_on(0)
    inv_u, inv_v = inverse_factors([sum_gram(1), gram_v])
    q_u = exact(qu_ref[...], inv_u, ((1,), (1,)))
    qu_ref[...] = q_u
    q_low = q_u.astype(BF)
    mine = qp.at[pl.ds(pl.multiple_of(f * half, half), half), :]
    mine[...] = jnp.concatenate([q_low[:half], q_low[half:]], axis=1)

    def low_copy(owner, d):
        piece = qp.at[pl.ds(pl.multiple_of(owner * half, half), half), :]
        return pltpu.make_async_remote_copy(src_ref=piece, dst_ref=piece, send_sem=q_send.at[d], recv_sem=q_recv.at[d],
                                            device_id=(lax.rem(f + d, nf), s), device_id_type=MESH)

    @pl.loop(1, nf)
    def _(d):
        low_copy(f, d).start()

    qv_ref[...] = exact(qv_ref[...], inv_v, ((1,), (1,)))
    pass_on(1)

    @pl.loop(2, line)
    def _(k):
        relay(k)

    for chunk in range(2, CHUNKS):
        pass_on(chunk)

    @pl.loop(1, nf)
    def _(d):
        low_copy(lax.rem(f + nf - d, nf), d).wait_recv()

    for i in range(nf):
        ql[i * rows : i * rows + half, :] = qp[i * half : (i + 1) * half, :R]
        ql[i * rows + half : (i + 1) * rows, :] = qp[i * half : (i + 1) * half, R:]

    for chunk in range(CHUNKS):
        token_copy(brother, chunk, brother, b_send, b_recv).wait_recv()
    far = lax.rem(brother + 2, ns)
    for chunk in range(CHUNKS):
        token_copy(far, chunk, brother, r_send, r_recv).wait_recv()

    @pl.loop(0, line)
    def _(at):
        pair_arrival(at).wait_recv()

    acc[...] = jnp.zeros_like(acc)
    sacc[...] = jnp.zeros_like(sacc)

    @pl.loop(0, D // KT)
    def _(t):
        at = pl.ds(pl.multiple_of(t * KT, KT), KT)
        piece = xs[:, at]
        acc[...] += dot(piece, ws[at, :], ((1,), (0,)))
        sacc[...] += dot(piece, ql[at, :], ((1,), (0,)))

    v_slice = qv_ref[pl.ds(pl.multiple_of(s * cols, cols), cols), :]
    offset = 2.0 * exact(sacc[...], v_slice, ((1,), (1,)))
    keys_ref[0] = (acc[...] + offset).astype(BF)
    keys_ref[1] = (acc[...] - offset).astype(BF)

    for turn in range(2):
        @pl.loop(1, nf)
        def _(d):
            gram_copy(turn, d).wait_send()

    @pl.loop(1, nf)
    def _(d):
        low_copy(f, d).wait_send()

    @pl.loop(1, line)
    def _(k):
        @pl.when((a + 1 < line) & (a - k + 1 >= 0))
        def _():
            up(k).wait_send()

        @pl.when((a > 0) & (a + k - 1 < line))
        def _():
            down(k).wait_send()

    @pl.loop(0, line)
    def _(at):
        pair(at).wait_send()

    for chunk in range(CHUNKS):
        token_copy(s, chunk, across, n_send, n_recv).wait_send()
        token_copy(s, chunk, brother, b_send, b_recv).wait_send()
        token_copy(across, chunk, brother, r_send, r_recv).wait_send()


def compute_keys(nf, ns, tokens, key_weight, u_factor, v_factor):
    length = tokens.shape[1] * ns
    rows, cols = key_weight.shape
    dma = lambda *n: pltpu.SemaphoreType.DMA(n)
    line = nf // 2
    return pl.pallas_call(
        functools.partial(keys_kernel, nf, ns),
        out_shape=(
            jax.ShapeDtypeStruct((2, length, cols), BF),
            jax.ShapeDtypeStruct((rows, R), F32),
            jax.ShapeDtypeStruct((KD, R), F32),
        ),
        in_specs=[ANY, ANY, VMEM, VMEM],
        out_specs=(VMEM, VMEM, VMEM),
        scratch_shapes=[
            pltpu.VMEM((length, D), BF),
            pltpu.VMEM((D, cols), BF),
            pltpu.VMEM((D // 2, 2 * R), BF),
            pltpu.VMEM((D, R), BF),
            pltpu.VMEM((2, nf, R, R), F32),
            pltpu.VMEM((length, cols), F32),
            pltpu.VMEM((length, R), F32),
            dma(2), dma(2, nf), dma(2, nf), dma(nf), dma(nf),
            dma(line + 1), dma(line + 1), dma(line + 1), dma(line + 1), dma(line), dma(line),
            dma(CHUNKS), dma(CHUNKS), dma(CHUNKS), dma(CHUNKS), dma(CHUNKS), dma(CHUNKS),
        ],
        compiler_params=pltpu.CompilerParams(collective_id=0, has_side_effects=True, vmem_limit_bytes=48 << 20),
        cost_estimate=pl.CostEstimate(flops=2 * length * D * (cols + R), bytes_accessed=16 << 20, transcendentals=0),
    )(tokens, key_weight, u_factor, v_factor)


def attention_kernel(heads, q_ref, k_ref, u_ref, v_ref, sums_ref, update_ref):
    step = pl.program_id(0)
    length = q_ref.shape[0]
    tile = 256
    scale = 1.0 / math.sqrt(HD)
    twice = scale * math.log2(math.e)

    @pl.when(step == 0)
    def _():
        sums_ref[...] = jnp.zeros_like(sums_ref)

    def parts(value):
        high = value.astype(BF)
        return high, (value - high.astype(F32)).astype(BF)

    u_high, u_rest = parts(u_ref[...])
    v_high, v_rest = parts(v_ref[...])
    product = dot(jnp.concatenate([u_high, u_rest, u_high], axis=1), jnp.concatenate([v_high, v_high, v_rest], axis=1), ((1,), (1,)))
    update_ref[...] = math.sqrt(D * KD / R) * product

    keep = lax.broadcasted_iota(jnp.int32, (tile, tile), 0) <= lax.broadcasted_iota(jnp.int32, (tile, tile), 1)
    for head in range(heads):
        for start in range(0, length, tile):
            q = q_ref[start : start + tile, head * HD : (head + 1) * HD]
            for p in range(2):
                last = dot(k_ref[p, start : start + tile, :], q, ((1,), (1,)))
                last = jnp.where(keep, last, -1e30)
                top = jnp.max(last, axis=0, keepdims=True)
                if start > 0:
                    before = dot(k_ref[p, :start, :], q, ((1,), (1,)))
                    top = jnp.maximum(top, jnp.max(before, axis=0, keepdims=True))
                total = jnp.sum(jnp.exp2((last - top) * twice), axis=0, keepdims=True)
                if start > 0:
                    total += jnp.sum(jnp.exp2((before - top) * twice), axis=0, keepdims=True)
                sums_ref[p : p + 1, start : start + tile] += top * scale + jnp.log(total)


def attend(query_rows, keys, q_u, q_v):
    length, width = query_rows.shape
    rows = q_u.shape[0]
    steps = 8
    heads = width // HD // steps
    return pl.pallas_call(
        functools.partial(attention_kernel, heads),
        grid=(steps,),
        out_shape=(jax.ShapeDtypeStruct((8, length), F32), jax.ShapeDtypeStruct((rows, KD), F32)),
        in_specs=[
            pl.BlockSpec((length, heads * HD), lambda i: (0, i)),
            pl.BlockSpec((2, length, HD), lambda i: (0, 0, i * heads // GROUP)),
            pl.BlockSpec((rows // steps, R), lambda i: (i, 0)),
            pl.BlockSpec((KD, R), lambda i: (0, 0)),
        ],
        out_specs=(pl.BlockSpec((8, length), lambda i: (0, 0)), pl.BlockSpec((rows // steps, KD), lambda i: (i, 0))),
        compiler_params=pltpu.CompilerParams(dimension_semantics=("arbitrary",), vmem_limit_bytes=32 << 20),
    )(query_rows, keys, q_u, q_v)


def loss_kernel(nf, ns, divisor, sums_ref, out_ref, over_f, over_s, f_send, f_recv, s_send, s_recv):
    f = lax.axis_index("fsdp")
    s = lax.axis_index("seq")
    barrier = pltpu.get_barrier_semaphore()

    @pl.loop(1, nf)
    def _(d):
        pl.semaphore_signal(barrier, inc=1, device_id=(lax.rem(f + d, nf), s), device_id_type=MESH)

    @pl.loop(1, ns)
    def _(d):
        pl.semaphore_signal(barrier, inc=1, device_id=(f, lax.rem(s + d, ns)), device_id_type=MESH)

    length = sums_ref.shape[1]
    over_s[s] = sum(sums_ref[:, at : at + 128] for at in range(0, length, 128))
    pl.semaphore_wait(barrier, nf - 1 + ns - 1)

    def copy_s(owner, d):
        return pltpu.make_async_remote_copy(src_ref=over_s.at[owner], dst_ref=over_s.at[owner], send_sem=s_send.at[d],
                                            recv_sem=s_recv.at[d], device_id=(f, lax.rem(s + d, ns)), device_id_type=MESH)

    def copy_f(owner, d):
        return pltpu.make_async_remote_copy(src_ref=over_f.at[owner], dst_ref=over_f.at[owner], send_sem=f_send.at[d],
                                            recv_sem=f_recv.at[d], device_id=(lax.rem(f + d, nf), s), device_id_type=MESH)

    @pl.loop(1, ns)
    def _(d):
        copy_s(s, d).start()

    @pl.loop(1, ns)
    def _(d):
        copy_s(lax.rem(s + ns - d, ns), d).wait_recv()

    over_f[f] = jnp.sum(over_s[...], axis=0)

    @pl.loop(1, nf)
    def _(d):
        copy_f(f, d).start()

    @pl.loop(1, nf)
    def _(d):
        copy_f(lax.rem(f + nf - d, nf), d).wait_recv()

    whole = jnp.sum(over_f[...], axis=0)
    out_ref[...] = jnp.broadcast_to(jnp.sum(whole, axis=1, keepdims=True) * (1.0 / divisor), out_ref.shape)

    @pl.loop(1, ns)
    def _(d):
        copy_s(s, d).wait_send()

    @pl.loop(1, nf)
    def _(d):
        copy_f(f, d).wait_send()


def total_loss(nf, ns, sums, divisor):
    dma = lambda n: pltpu.SemaphoreType.DMA((n,))
    return pl.pallas_call(
        functools.partial(loss_kernel, nf, ns, divisor),
        out_shape=jax.ShapeDtypeStruct((8, 128), F32),
        in_specs=[VMEM],
        out_specs=VMEM,
        scratch_shapes=[pltpu.VMEM((nf, 8, 128), F32), pltpu.VMEM((ns, 8, 128), F32), dma(nf), dma(nf), dma(ns), dma(ns)],
        compiler_params=pltpu.CompilerParams(collective_id=1, has_side_effects=True),
    )(sums)


def solution(mesh):
    nf, ns = mesh.shape["fsdp"], mesh.shape["seq"]

    def local(tokens, queries, key_weight, u_factor, v_factor):
        length = tokens.shape[1] * ns
        keys, q_u, q_v = compute_keys(nf, ns, tokens, key_weight, u_factor, v_factor)
        sums, update = attend(queries[0], keys, q_u, q_v)
        losses = total_loss(nf, ns, sums, float(nf * length * HQ))
        return update, losses[:2, 0]

    in_specs = (
        P("fsdp", "seq", None),
        P("fsdp", None, "seq"),
        P("fsdp", "seq"),
        P("fsdp", None),
        P(),
    )
    out_specs = (P("fsdp", None), P())
    return jax.shard_map(local, mesh=mesh, in_specs=in_specs, out_specs=out_specs, check_vma=False)
```

time: 402 us -> 117 us (0.29)
  waiting for transfers between devices: 241 us -> 0 us
  Pallas kernels: 0 us -> 109 us
  other arithmetic: 60.3 us -> 0 us
  matrix products: 39.7 us -> 0 us
  blocking collectives: 38.5 us -> 0 us
  between operations: 14 us -> 0.68 us
    all_gather x5 -> x0, waiting for transfers between devices: 239 us -> none  [the longest x2 102 us: local(): whole_u = lax.all_gather(u_rows, 'fsdp', axis=0, tiled=True)]
    pallas_call x0 -> x3, Pallas kernels: none -> 109 us  [the longest x1 86.8 us: compute_keys(): pl.pallas_call(functools.partial(keys_kernel, nf, ns), out_shape=(jax.Sha...]
    another operation x23 -> x0, other arithmetic: 48.3 us -> none  [the longest x12 26.1 us: solve_rows(): lower = jnp.linalg.cholesky(gram)]
    psum x1 -> x0, blocking collectives: 38.5 us -> none  [local(): sums = lax.psum(partial_sums, ('fsdp', 'seq'))]
    dot_general x24 -> x0, matrix products: 36.7 us -> none  [the longest x6 14.5 us: highest(): jnp.dot(left, right, precision=lax.Precision.HIGHEST, preferred_element_t...]
    reduce_sum x35 -> x0, other arithmetic: 11.3 us -> none  [the longest x16 9.22 us: one_query_head(): jnp.sum(jnp.where(causal[None], jnp.exp(scores - top[..., None]), 0.0), a...]
  transfers between devices with their start and end apart: 5 -> 0, of which waited for: 5 -> 0; matrix products, arithmetic and copies ran while one was open for 9% -> 0% of each run, Pallas kernels for 0% -> 0%
where the time goes in v1:
time: 117 us; the launch traced here: 116 us
  Pallas kernels  109 us (93%)
  local copies, waits for them, and re-layouts  6.83 us (6%)
    pallas_call x1, Pallas kernels, compute_keys(): pl.pallas_call(functools.partial(keys_kernel, nf, ns), out_shape=(jax.Sha...  86.8 us
    pallas_call x1, Pallas kernels, total_loss(): pl.pallas_call(functools.partial(loss_kernel, nf, ns, divisor), out_shape...  12.6 us
    pallas_call x1, Pallas kernels, attend(): pl.pallas_call(functools.partial(attention_kernel, heads), grid=(steps,),...  9.57 us
    unnamed x10, local copies, waits for them, and re-layouts  5.52 us

profile of v1, /device:TPU:0, one launch (start us, length us, event | category | flops | bytes accessed | tf_op | source)
XLA Modules:
  0.0 116.4 jit_solution(12855007270026300311)
XLA Ops:
  0.6 1.1 copy.9.u_ref
  1.8 1.1 copy.10.v_ref
  2.9 0.0 copy-start.2
  2.9 1.6 %copy-done.2 = bf16[1,128,8192]{2,1,0:T(8,128)(2,1)S(1)} copy-done((bf16[1,128,8192]{2,1,0:T(8,128)(2,1)S(1)}, bf16[1,128,8192]{2,1,0:T(8,128)(2,1)}, u32[]{:S(2)}) %copy-start.2) | copy-done | bytes 2097176
  4.5 0.0 copy-start.3
  4.5 1.0 copy-done.3
  5.6 0.0 copy-start
  5.6 86.8 %shard_map.68 = (bf16[2,512,256]{2,1,0:T(8,128)(2,1)S(1)}, f32[1024,64]{1,0:T(8,128)S(1)}, f32[1024,64]{1,0:T(8,128)S(1)}) custom-call(bf16[1,128,8192]{2,1,0:T(8,128)(2,1)S(1)} %copy-done.2, bf16[1024,256]{1,0:T(8,128)(2,1)S(1)} %copy-done.3, f32[1024,64]{1,0:T(8,128)S(1)} %copy.9.u_ref, f32[1024,64]{1,0:T(8,128)S(1)} %copy.10.v_ref), custom_call_target="tpu_custom_call" | custom-call | flops 2684354560 | bytes 16777216 | tf_op jit(solution)/shard_map/pallas_call | solution.py:291
  92.4 0.0 copy-done
  92.4 9.6 %shard_map.69 = (f32[8,512]{1,0:T(8,128)S(1)}, f32[1024,1024]{1,0:T(8,128)}) custom-call(bf16[512,2048]{1,0:T(8,128)(2,1)S(1)} %bitcast.1, bf16[2,512,256]{2,1,0:T(8,128)(2,1)S(1)} %get-tuple-element.7.k_ref, f32[1024,64]{1,0:T(8,128)S(1)} %get-tuple-element.8.u_ref, f32[1024,64]{1,0:T(8,128)S(1)} %get-tuple-element.9.v_ref), custom_call_target="tpu_custom_call" | custom-call | tf_op jit(solution)/shard_map/pallas_call | solution.py:359
  102.0 0.0 copy-start.1
  102.0 0.6 copy-done.1
  102.5 12.6 %shard_map.70 = f32[8,128]{1,0:T(8,128)} custom-call(f32[8,512]{1,0:T(8,128)} %copy-done.1), custom_call_target="tpu_custom_call" | custom-call | tf_op jit(solution)/shard_map/pallas_call | solution.py:431
  115.1 1.3 %slice_reduce_fusion = f32[2]{0:T(128)} fusion(f32[8,128]{1,0:T(8,128)} %shard_map.70), kind=kLoop, calls=%fused_computation | loop fusion | bytes 16 | tf_op jit(solution)/shard_map/slice | solution.py:449
Async XLA Ops:
  2.9 1.6 %copy-start.2 = (bf16[1,128,8192]{2,1,0:T(8,128)(2,1)S(1)}, bf16[1,128,8192]{2,1,0:T(8,128)(2,1)}, u32[]{:S(2)}) copy-start(bf16[1,128,8192]{2,1,0:T(8,128)(2,1)} %x_hbm.1) | copy-start | bytes 6291460
  4.5 1.0 copy-start.3
  5.6 86.8 %copy-start = (bf16[1,512,2048]{2,1,0:T(8,128)(2,1)S(1)}, bf16[1,512,2048]{2,1,0:T(8,128)(2,1)}, u32[]{:S(2)}) copy-start(bf16[1,512,2048]{2,1,0:T(8,128)(2,1)} %param.6) | copy-start | bytes 6291460
  102.0 0.6 copy-start.1

commit v2 on v1

--- a/solution.py
+++ b/solution.py
@@ -50,9 +50,9 @@
     return [(a * lax.rsqrt(s))[:, R:] for a, s in zip(work, scales)]
 
 
-def keys_kernel(nf, ns, x_hbm, w_hbm, u_ref, v_ref, keys_ref, qu_ref, qv_ref, xs, ws, qp, ql, gm, acc, sacc,
+def keys_kernel(nf, ns, x_hbm, w_hbm, u_ref, v_ref, keys_ref, qu_ref, qv_ref, xs, ws, qt, ql, ut, vt, gm, acc, sacc,
                 in_sem, g_send, g_recv, q_send, q_recv, up_send, up_recv, dn_send, dn_recv, p_send, p_recv,
-                b_send, b_recv, n_send, n_recv, r_send, r_recv):
+                b_send, b_recv, n_send, n_recv, r_send, r_recv, l_send, l_recv):
     f = lax.axis_index("fsdp")
     s = lax.axis_index("seq")
     line = nf // 2
@@ -61,8 +61,9 @@
     core = lax.rem(s, 2)
     brother = s - core + (1 - core)
     across = lax.rem(s + 2, ns)
-    rows = u_ref.shape[0]
-    half = rows // 2
+    rows = u_ref.shape[1]
+    share, _, _, part = qt.shape
+    own = s if share > 1 else 0
     plen = xs.shape[0] // ns
     width = D // CHUNKS
     cols = ws.shape[1]
@@ -82,8 +83,6 @@
     def _(d):
         pl.semaphore_signal(barrier, inc=1, device_id=(f, lax.rem(s + d, ns)), device_id_type=MESH)
 
-    gram_v = exact(v_ref[...], v_ref[...], ((0,), (0,)))
-    gram_u = exact(u_ref[...], u_ref[...], ((0,), (0,)))
     pl.semaphore_wait(barrier, nf - 1 + ns - 1)
 
     def gram_copy(turn, d):
@@ -178,60 +177,81 @@
         token_copy(across, chunk, across, n_send, n_recv).wait_recv()
         token_copy(across, chunk, brother, r_send, r_recv).start()
 
-    send_gram(0, gram_u)
     load_w.wait()
     sends(1)
     pair(a).start()
     load_x.wait()
     for chunk in range(CHUNKS):
         token_copy(s, chunk, across, n_send, n_recv).start()
+    send_gram(0, exact(u_ref[...], u_ref[...], ((1,), (1,))))
     for chunk in range(CHUNKS):
         token_copy(s, chunk, brother, b_send, b_recv).start()
 
+    gram_v = exact(v_ref[...], v_ref[...], ((1,), (1,)))
     inv_u, inv_v = inverse_factors([sum_gram(0), gram_v])
-    qu_ref[...] = exact(u_ref[...], inv_u, ((1,), (1,)))
-    send_gram(1, exact(qu_ref[...], qu_ref[...], ((0,), (0,))))
-    qv_ref[...] = exact(v_ref[...], inv_v, ((1,), (1,)))
-    gram_v = exact(qv_ref[...], qv_ref[...], ((0,), (0,)))
+    ut[...] = exact(inv_u, u_ref[...], ((1,), (0,)))
+    send_gram(1, exact(ut[...], ut[...], ((1,), (1,))))
+    vt[...] = exact(inv_v, v_ref[...], ((1,), (0,)))
+    gram_v = exact(vt[...], vt[...], ((1,), (1,)))
     relay(1)
     pass_on(0)
     inv_u, inv_v = inverse_factors([sum_gram(1), gram_v])
-    q_u = exact(qu_ref[...], inv_u, ((1,), (1,)))
-    qu_ref[...] = q_u
-    q_low = q_u.astype(BF)
-    mine = qp.at[pl.ds(pl.multiple_of(f * half, half), half), :]
-    mine[...] = jnp.concatenate([q_low[:half], q_low[half:]], axis=1)
+    ut[...] = exact(inv_u, ut[...], ((1,), (0,)))
+    for j in range(share):
+        @pl.when(own == j)
+        def _():
+            qt[j, f] = ut[:, j * part : (j + 1) * part].astype(BF)
 
     def low_copy(owner, d):
-        piece = qp.at[pl.ds(pl.multiple_of(owner * half, half), half), :]
+        piece = qt.at[own, owner]
         return pltpu.make_async_remote_copy(src_ref=piece, dst_ref=piece, send_sem=q_send.at[d], recv_sem=q_recv.at[d],
                                             device_id=(lax.rem(f + d, nf), s), device_id_type=MESH)
 
+    def share_copy(owner, at, to):
+        piece = qt.at[owner]
+        return pltpu.make_async_remote_copy(src_ref=piece, dst_ref=piece, send_sem=l_send.at[at], recv_sem=l_recv.at[at],
+                                            device_id=(f, to), device_id_type=MESH)
+
     @pl.loop(1, nf)
     def _(d):
         low_copy(f, d).start()
 
-    qv_ref[...] = exact(qv_ref[...], inv_v, ((1,), (1,)))
+    vt[...] = exact(inv_v, vt[...], ((1,), (0,)))
+    qu_ref[...] = ut[...].T
+    qv_ref[...] = vt[...].T
     pass_on(1)
-
-    @pl.loop(2, line)
+    if line > 2:
+        relay(2)
+
+    @pl.loop(1, nf)
+    def _(d):
+        low_copy(lax.rem(f + nf - d, nf), d).wait_recv()
+
+    if share > 1:
+        share_copy(own, 0, across).start()
+        share_copy(own, 1, brother).start()
+
+    @pl.loop(3, line)
     def _(k):
         relay(k)
 
-    for chunk in range(2, CHUNKS):
-        pass_on(chunk)
-
-    @pl.loop(1, nf)
-    def _(d):
-        low_copy(lax.rem(f + nf - d, nf), d).wait_recv()
-
+    pass_on(2)
+    if share > 1:
+        share_copy(across, 0, across).wait_recv()
+        share_copy(across, 2, brother).start()
+    pass_on(3)
+
+    far = lax.rem(brother + 2, ns)
+    if share > 1:
+        share_copy(brother, 1, brother).wait_recv()
+        share_copy(far, 2, brother).wait_recv()
     for i in range(nf):
-        ql[i * rows : i * rows + half, :] = qp[i * half : (i + 1) * half, :R]
-        ql[i * rows + half : (i + 1) * rows, :] = qp[i * half : (i + 1) * half, R:]
+        for j in range(share):
+            at = i * rows + j * part
+            ql[:, at : at + part] = qt[j, i]
 
     for chunk in range(CHUNKS):
         token_copy(brother, chunk, brother, b_send, b_recv).wait_recv()
-    far = lax.rem(brother + 2, ns)
     for chunk in range(CHUNKS):
         token_copy(far, chunk, brother, r_send, r_recv).wait_recv()
 
@@ -247,10 +267,10 @@
         at = pl.ds(pl.multiple_of(t * KT, KT), KT)
         piece = xs[:, at]
         acc[...] += dot(piece, ws[at, :], ((1,), (0,)))
-        sacc[...] += dot(piece, ql[at, :], ((1,), (0,)))
-
-    v_slice = qv_ref[pl.ds(pl.multiple_of(s * cols, cols), cols), :]
-    offset = 2.0 * exact(sacc[...], v_slice, ((1,), (1,)))
+        sacc[...] += dot(piece, ql[:, at], ((1,), (1,)))
+
+    v_slice = vt[:, pl.ds(pl.multiple_of(s * cols, cols), cols)]
+    offset = 2.0 * exact(sacc[...], v_slice, ((1,), (0,)))
     keys_ref[0] = (acc[...] + offset).astype(BF)
     keys_ref[1] = (acc[...] - offset).astype(BF)
 
@@ -281,6 +301,10 @@
         token_copy(s, chunk, across, n_send, n_recv).wait_send()
         token_copy(s, chunk, brother, b_send, b_recv).wait_send()
         token_copy(across, chunk, brother, r_send, r_recv).wait_send()
+    if share > 1:
+        share_copy(own, 0, across).wait_send()
+        share_copy(own, 1, brother).wait_send()
+        share_copy(across, 2, brother).wait_send()
 
 
 def compute_keys(nf, ns, tokens, key_weight, u_factor, v_factor):
@@ -288,6 +312,7 @@
     rows, cols = key_weight.shape
     dma = lambda *n: pltpu.SemaphoreType.DMA(n)
     line = nf // 2
+    share = ns if rows % (128 * ns) == 0 else 1
     return pl.pallas_call(
         functools.partial(keys_kernel, nf, ns),
         out_shape=(
@@ -300,18 +325,20 @@
         scratch_shapes=[
             pltpu.VMEM((length, D), BF),
             pltpu.VMEM((D, cols), BF),
-            pltpu.VMEM((D // 2, 2 * R), BF),
-            pltpu.VMEM((D, R), BF),
+            pltpu.VMEM((share, nf, R, rows // share), BF),
+            pltpu.VMEM((R, D), BF),
+            pltpu.VMEM((R, rows), F32),
+            pltpu.VMEM((R, KD), F32),
             pltpu.VMEM((2, nf, R, R), F32),
             pltpu.VMEM((length, cols), F32),
             pltpu.VMEM((length, R), F32),
             dma(2), dma(2, nf), dma(2, nf), dma(nf), dma(nf),
             dma(line + 1), dma(line + 1), dma(line + 1), dma(line + 1), dma(line), dma(line),
-            dma(CHUNKS), dma(CHUNKS), dma(CHUNKS), dma(CHUNKS), dma(CHUNKS), dma(CHUNKS),
+            dma(CHUNKS), dma(CHUNKS), dma(CHUNKS), dma(CHUNKS), dma(CHUNKS), dma(CHUNKS), dma(3), dma(3),
         ],
-        compiler_params=pltpu.CompilerParams(collective_id=0, has_side_effects=True, vmem_limit_bytes=48 << 20),
+        compiler_params=pltpu.CompilerParams(collective_id=0, has_side_effects=True, vmem_limit_bytes=60 << 20),
         cost_estimate=pl.CostEstimate(flops=2 * length * D * (cols + R), bytes_accessed=16 << 20, transcendentals=0),
-    )(tokens, key_weight, u_factor, v_factor)
+    )(tokens, key_weight, u_factor.T, v_factor.T)
 
 
 def attention_kernel(heads, q_ref, k_ref, u_ref, v_ref, sums_ref, update_ref):

time: 117 us -> 110 us (0.940)
  Pallas kernels: 109 us -> 104 us
  local copies, waits for them, and re-layouts: 6.83 us -> 5.03 us
    pallas_call x1, Pallas kernels: 86.8 us -> 82.7 us  [compute_keys(): pl.pallas_call(functools.partial(keys_kernel, nf, ns), out_shape=(jax.Sha...]
    unnamed x10, local copies, waits for them, and re-layouts: 5.52 us -> 3.72 us
    pallas_call x1, Pallas kernels: 12.6 us -> 11.3 us  [total_loss(): pl.pallas_call(functools.partial(loss_kernel, nf, ns, divisor), out_shape...]
where the time goes in v2:
time: 110 us; the launch traced here: 109 us
  Pallas kernels  104 us (95%)
  local copies, waits for them, and re-layouts  5.03 us (5%)
    pallas_call x1, Pallas kernels, compute_keys(): pl.pallas_call(functools.partial(keys_kernel, nf, ns), out_shape=(jax.Sha...  82.7 us
    pallas_call x1, Pallas kernels, total_loss(): pl.pallas_call(functools.partial(loss_kernel, nf, ns, divisor), out_shape...  11.3 us
    pallas_call x1, Pallas kernels, attend(): pl.pallas_call(functools.partial(attention_kernel, heads), grid=(steps,),...  9.54 us
    unnamed x10, local copies, waits for them, and re-layouts  3.72 us

profile of v2, /device:TPU:0, one launch (start us, length us, event | category | flops | bytes accessed | tf_op | source)
XLA Modules:
  0.0 109.3 jit_solution(16080810284272265355)
XLA Ops:
  0.6 0.0 copy-start
  0.6 82.7 %shard_map.68 = (bf16[2,512,256]{2,1,0:T(8,128)(2,1)}, f32[1024,64]{1,0:T(8,128)}, f32[1024,64]{1,0:T(8,128)}) custom-call(bf16[1,128,8192]{2,1,0:T(8,128)(2,1)} %x_hbm.1, bf16[1024,256]{1,0:T(8,128)(2,1)} %w_hbm.1, f32[64,1024]{1,0:T(8,128)} %bitcast.4, f32[64,1024]{1,0:T(8,128)} %bitcast.5), custom_call_target="tpu_custom_call" | custom-call | flops 2684354560 | bytes 16777216 | tf_op jit(solution)/shard_map/pallas_call | solution.py:316
  83.4 0.0 copy-done
  83.4 0.0 copy-start.1
  83.4 1.0 copy-done.1
  84.4 0.0 copy-start.2
  84.4 1.0 copy-done.2
  85.5 0.0 copy-start.3
  85.5 1.0 copy-done.3
  86.5 9.5 %shard_map.69 = (f32[8,512]{1,0:T(8,128)S(1)}, f32[1024,1024]{1,0:T(8,128)}) custom-call(bf16[512,2048]{1,0:T(8,128)(2,1)S(1)} %bitcast.3, bf16[2,512,256]{2,1,0:T(8,128)(2,1)S(1)} %copy-done.1, f32[1024,64]{1,0:T(8,128)S(1)} %copy-done.2, f32[1024,64]{1,0:T(8,128)S(1)} %copy-done.3), custom_call_target="tpu_custom_call" | custom-call | tf_op jit(solution)/shard_map/pallas_call | solution.py:386
  96.1 0.0 copy-start.4
  96.1 0.6 copy-done.4
  96.7 11.3 %shard_map.70 = f32[8,128]{1,0:T(8,128)} custom-call(f32[8,512]{1,0:T(8,128)} %copy-done.4), custom_call_target="tpu_custom_call" | custom-call | tf_op jit(solution)/shard_map/pallas_call | solution.py:458
  108.0 1.3 %slice_reduce_fusion = f32[2]{0:T(128)} fusion(f32[8,128]{1,0:T(8,128)} %shard_map.70), kind=kLoop, calls=%fused_computation | loop fusion | bytes 16 | tf_op jit(solution)/shard_map/slice | solution.py:476
Async XLA Ops:
  0.6 82.7 %copy-start = (bf16[1,512,2048]{2,1,0:T(8,128)(2,1)S(1)}, bf16[1,512,2048]{2,1,0:T(8,128)(2,1)}, u32[]{:S(2)}) copy-start(bf16[1,512,2048]{2,1,0:T(8,128)(2,1)} %param.6) | copy-start | bytes 6291460
  83.4 1.0 copy-start.1
  84.4 1.0 copy-start.2
  85.5 1.0 copy-start.3
  96.1 0.6 copy-start.4

commit v3 on v2

--- a/solution.py
+++ b/solution.py
@@ -194,7 +194,6 @@
     vt[...] = exact(inv_v, v_ref[...], ((1,), (0,)))
     gram_v = exact(vt[...], vt[...], ((1,), (1,)))
     relay(1)
-    pass_on(0)
     inv_u, inv_v = inverse_factors([sum_gram(1), gram_v])
     ut[...] = exact(inv_u, ut[...], ((1,), (0,)))
     for j in range(share):
@@ -219,9 +218,10 @@
     vt[...] = exact(inv_v, vt[...], ((1,), (0,)))
     qu_ref[...] = ut[...].T
     qv_ref[...] = vt[...].T
-    pass_on(1)
     if line > 2:
         relay(2)
+    pass_on(0)
+    pass_on(1)
 
     @pl.loop(1, nf)
     def _(d):
@@ -394,7 +394,7 @@
             pl.BlockSpec((KD, R), lambda i: (0, 0)),
         ],
         out_specs=(pl.BlockSpec((8, length), lambda i: (0, 0)), pl.BlockSpec((rows // steps, KD), lambda i: (i, 0))),
-        compiler_params=pltpu.CompilerParams(dimension_semantics=("arbitrary",), vmem_limit_bytes=32 << 20),
+        compiler_params=pltpu.CompilerParams(dimension_semantics=("arbitrary",), vmem_limit_bytes=60 << 20),
     )(query_rows, keys, q_u, q_v)
 
 

time: 110 us -> 107 us (0.973)
  local copies, waits for them, and re-layouts: 5.03 us -> 1.31 us
    unnamed x10 -> x0, local copies, waits for them, and re-layouts: 3.72 us -> none
    pallas_call x1, Pallas kernels: 9.54 us -> 10.9 us  [attend(): pl.pallas_call(functools.partial(attention_kernel, heads), grid=(steps,),...]
where the time goes in v3:
time: 107 us
  Pallas kernels  105 us (98%)
  local copies, waits for them, and re-layouts  1.31 us (1%)
    pallas_call x1, Pallas kernels, compute_keys(): pl.pallas_call(functools.partial(keys_kernel, nf, ns), out_shape=(jax.Sha...  82.6 us
    pallas_call x1, Pallas kernels, total_loss(): pl.pallas_call(functools.partial(loss_kernel, nf, ns, divisor), out_shape...  11.3 us
    pallas_call x1, Pallas kernels, attend(): pl.pallas_call(functools.partial(attention_kernel, heads), grid=(steps,),...  10.9 us

profile of v3, /device:TPU:0, one launch (start us, length us, event | category | flops | bytes accessed | tf_op | source)
XLA Modules:
  0.0 106.7 jit_solution(11455672963504892290)
XLA Ops:
  0.6 82.6 %shard_map.68 = (bf16[2,512,256]{2,1,0:T(8,128)(2,1)}, f32[1024,64]{1,0:T(8,128)}, f32[1024,64]{1,0:T(8,128)}) custom-call(bf16[1,128,8192]{2,1,0:T(8,128)(2,1)} %x_hbm.1, bf16[1024,256]{1,0:T(8,128)(2,1)} %w_hbm.1, f32[64,1024]{1,0:T(8,128)} %bitcast.4, f32[64,1024]{1,0:T(8,128)} %bitcast.5), custom_call_target="tpu_custom_call" | custom-call | flops 2684354560 | bytes 16777216 | tf_op jit(solution)/shard_map/pallas_call | solution.py:316
  83.2 10.9 %shard_map.69 = (f32[8,512]{1,0:T(8,128)}, f32[1024,1024]{1,0:T(8,128)}) custom-call(bf16[512,2048]{1,0:T(8,128)(2,1)} %bitcast.3, bf16[2,512,256]{2,1,0:T(8,128)(2,1)} %get-tuple-element.7.k_ref, f32[1024,64]{1,0:T(8,128)} %get-tuple-element.8.u_ref, f32[1024,64]{1,0:T(8,128)} %get-tuple-element.9.v_ref), custom_call_target="tpu_custom_call" | custom-call | tf_op jit(solution)/shard_map/pallas_call | solution.py:386
  94.1 11.3 %shard_map.70 = f32[8,128]{1,0:T(8,128)} custom-call(f32[8,512]{1,0:T(8,128)} %get-tuple-element.11.sums_ref), custom_call_target="tpu_custom_call" | custom-call | tf_op jit(solution)/shard_map/pallas_call | solution.py:458
  105.4 1.3 %slice_reduce_fusion = f32[2]{0:T(128)} fusion(f32[8,128]{1,0:T(8,128)} %shard_map.70), kind=kLoop, calls=%fused_computation | loop fusion | bytes 16 | tf_op jit(solution)/shard_map/slice | solution.py:476
